TPU v7x, 32 devices: a whole 2x2x4 slice. The times are simulated.
32 devices in a mesh: col: 4 (over y, x), gz: 8 (over z, core).
Axes of the slice: x: 2, y: 2, z: 4, core: 2. Of those that a mesh axis runs over, the one named last changes fastest.
Arguments:
- segments: float32 [9, 98304], P(None, ('col', 'gz')), may hold values from -6 to 6
- node_owner: int32 [2, 98304], P(None, ('col', 'gz')), may hold values from 0 to 4
- node_slot: int32 [2, 98304], P(None, ('col', 'gz')), may hold values from 0 to 3071
- pair_first: int32 [10240], P(('col', 'gz')), may hold values from 0 to 23
- pair_second: int32 [10240], P(('col', 'gz')), may hold values from 0 to 71
- pair_count: int32 [32], P(('col', 'gz')), may hold values from 106 to 320, as said below
Outputs:
- node_force: float32 [3, 98304], P(None, ('col', 'gz'))
Inputs may be any that keep to these rules, and one draw needn't show every extreme that they name: `pair_count`: each device has at least 106 listed pairs (a third, rounded down), and some device has exactly 320; entries past a device's count are ignored.
All inputs are finite; a program needn't handle non-finite values.
Results may differ from a plain program's by a relative error of at most 0.0003.
Values sent between devices are 32-bit elements; how exact they have to be, the bound alone decides.
No kernel may reach another device: no remote copies, remote signals or barrier semaphores. Data moves between devices by JAX's collectives and lax.ppermute only.
A program may use at most 64 MiB of HBM per device.

v0:
```python
import jax
import jax.numpy as jnp
from jax import lax
from jax.sharding import PartitionSpec as P

BLK = 128
GROUP = 32
NODE_DEV = 3072


MU = 0.02
CORE_SQ = 0.5


def extended(value, sides, width):
    for axis, dim in sides:
        peers, length = (lax.axis_size(axis), value.shape[dim])
        up = [(i, (i + 1) % peers) for i in range(peers)]
        down = [(j, i) for i, j in up]
        last = lax.slice_in_dim(value, length - width, length, axis=dim)
        first = lax.slice_in_dim(value, 0, width, axis=dim)
        before = lax.ppermute(last, axis, up)
        after = lax.ppermute(first, axis, down)
        value = jnp.concatenate([before, value, after], axis=dim)
    return value


def pair_tile(first_block, second_block):
    first_pos = first_block[0:3]
    second_pos = second_block[0:3]
    offset = first_pos[:, :, None] - second_pos[:, None, :]
    radius_sq = jnp.sum(offset * offset, axis=0) + CORE_SQ
    inverse = lax.rsqrt(radius_sq)
    burgers = jnp.dot(
        first_block[3:6].T,
        second_block[3:6],
        precision=lax.Precision.HIGHEST,
        preferred_element_type=jnp.float32,
    )
    tangents = jnp.dot(
        first_block[6:9].T,
        second_block[6:9],
        precision=lax.Precision.HIGHEST,
        preferred_element_type=jnp.float32,
    )
    coupling = MU * burgers * tangents * (inverse * inverse * inverse)
    pulled = jnp.einsum("kj,ij->ki", second_pos, coupling, precision=lax.Precision.HIGHEST)
    return first_pos * jnp.sum(coupling, axis=1)[None, :] - pulled


def run_pairs(segments, source, shift_blocks, pair_first, pair_second, order, start, stop, forces):
    list_length = pair_first.shape[0]
    source_blocks = source.shape[1] // BLK
    rounds = (stop - start + GROUP - 1) // GROUP

    def one_round(round_index, totals):
        positions = start + round_index * GROUP + jnp.arange(GROUP, dtype=jnp.int32)
        active = (positions < stop).astype(jnp.float32)
        picked = order[jnp.minimum(positions, list_length - 1)]
        firsts = pair_first[picked]
        seconds = jnp.clip(pair_second[picked] - shift_blocks, 0, source_blocks - 1)
        first_blocks = jax.vmap(
            lambda block_index: lax.dynamic_slice_in_dim(segments, block_index * BLK, BLK, 1)
        )(firsts)
        second_blocks = jax.vmap(
            lambda block_index: lax.dynamic_slice_in_dim(source, block_index * BLK, BLK, 1)
        )(seconds)
        tile_forces = jax.vmap(pair_tile)(first_blocks, second_blocks) * active[:, None, None]
        return totals.at[:, firsts].add(jnp.transpose(tile_forces, (1, 0, 2)))

    return lax.fori_loop(0, rounds, one_round, forces)


def fetch_window(segments):
    return extended(segments, (("gz", 1),), segments.shape[1])


def on_device(segments, node_owner, node_slot, pair_first, pair_second, pair_count):
    seg_width = segments.shape[1]
    blocks = seg_width // BLK
    list_length = pair_first.shape[0]
    pair_total = pair_count[0]
    forces = jnp.zeros((3, blocks, BLK), jnp.float32)
    order = jnp.arange(list_length, dtype=jnp.int32)
    window = fetch_window(segments)
    forces = run_pairs(segments, window, 0, pair_first, pair_second, order, 0, pair_total, forces)
    halved = 0.5 * forces.reshape(3, seg_width)
    columns = lax.axis_size("col")
    stride = columns // 4
    column = lax.axis_index("col")

    def target(codes):
        moved = jnp.where(codes == 1, 1, 0) + jnp.where(codes == 2, -1, 0)
        moved = moved + jnp.where(codes == 3, stride, 0) + jnp.where(codes == 4, -stride, 0)
        return (column + moved) % columns

    buffer = jnp.zeros((3, columns * NODE_DEV), jnp.float32)
    buffer = buffer.at[:, target(node_owner[0]) * NODE_DEV + node_slot[0]].add(halved)
    buffer = buffer.at[:, target(node_owner[1]) * NODE_DEV + node_slot[1]].add(halved)
    received = lax.all_to_all(
        buffer.reshape(3, columns, NODE_DEV), "col", split_axis=1, concat_axis=1, tiled=True
    )
    node_total = jnp.sum(received, axis=1)
    return node_total


def solution(mesh):
    in_specs = (
        P(None, ("col", "gz")),
        P(None, ("col", "gz")),
        P(None, ("col", "gz")),
        P(("col", "gz")),
        P(("col", "gz")),
        P(("col", "gz")),
    )
    out_specs = P(None, ("col", "gz"))
    return jax.shard_map(
        on_device, mesh=mesh, in_specs=in_specs, out_specs=out_specs, check_vma=False
    )
```

profile of v0, /device:TPU:0, one launch (start us, length us, event | category | flops | bytes accessed | tf_op | source)
XLA Modules:
  0.0 1280.4 jit_solution(4137360935917556106)
XLA Ops:
  0.0 4.5 collective-permute-start.1
  6.2 1.9 collective-permute-done.1
  8.1 3.5 collective-permute-done
  12.6 970.7 %while.19 = (s32[]{:T(128)}, f32[3,24,128]{2,0,1:T(4,128)S(1)}, s32[]{:T(128)}, s32[320]{0:T(512)}, f32[9,3072]{1,0:T(8,128)}, /*index=5*/s32[320]{0:T(512)}, f3...) while((s32[]{:T(128)}, f32[3,24,128]{2,0,1:T(4,128)S(1)}, ...), condition=%wide.region_4.5_spmd.clone, body=%wide.region_0.4_spmd.clone.sunk | while | flops 64535272 | bytes 18032736 | solution.py:71
  16.9 39.0 %while.20 = (s32[]{:T(128)}, f32[9,9216]{1,0:T(8,128)S(1)}, s32[32,2]{0,1:T(2,128)S(1)}, f32[32,9,128]{2,1,0:T(8,128)S(1)}, s32[]{:T(128)}) while((s32[]{:T(128)}, f32[9,9216]{1,0:T(8,128)S(1)}, s32[32,2]{0,1:T(2,128)S(1)}, f32[32,9,128]{2,1,0:T(8,128)S(1)}, s32[]{:T(128)}) %tuple.60), condition=%wide.while_cond.1, body=%wide.while_body.1.sunk | while | flops 2 | bytes 16489 | solution.py:66
  55.9 62.0 %while.21 = (s32[]{:T(128)}, f32[9,3072]{1,0:T(8,128)}, s32[32,2]{0,1:T(2,128)S(1)}, f32[32,9,128]{2,1,0:T(8,128)S(1)}, s32[]{:T(128)}) while((s32[]{:T(128)}, f32[9,3072]{1,0:T(8,128)}, s32[32,2]{0,1:T(2,128)S(1)}, f32[32,9,128]{2,1,0:T(8,128)S(1)}, s32[]{:T(128)}) %tuple.63), condition=%wide.while_cond, body=%wide.while_body.sunk | while | flops 2 | bytes 12905 | solution.py:63
  117.9 3.4 multiply_reduce_fusion.2
  123.2 3.4 fusion.48
  126.7 3.6 fusion.49
  138.2 39.0 %while.20 = (s32[]{:T(128)}, f32[9,9216]{1,0:T(8,128)S(1)}, s32[32,2]{0,1:T(2,128)S(1)}, f32[32,9,128]{2,1,0:T(8,128)S(1)}, s32[]{:T(128)}) while((s32[]{:T(128)}, f32[9,9216]{1,0:T(8,128)S(1)}, s32[32,2]{0,1:T(2,128)S(1)}, f32[32,9,128]{2,1,0:T(8,128)S(1)}, s32[]{:T(128)}) %tuple.60), condition=%wide.while_cond.1, body=%wide.while_body.1.sunk | while | flops 2 | bytes 16489 | solution.py:66
  177.2 62.0 %while.21 = (s32[]{:T(128)}, f32[9,3072]{1,0:T(8,128)}, s32[32,2]{0,1:T(2,128)S(1)}, f32[32,9,128]{2,1,0:T(8,128)S(1)}, s32[]{:T(128)}) while((s32[]{:T(128)}, f32[9,3072]{1,0:T(8,128)}, s32[32,2]{0,1:T(2,128)S(1)}, f32[32,9,128]{2,1,0:T(8,128)S(1)}, s32[]{:T(128)}) %tuple.63), condition=%wide.while_cond, body=%wide.while_body.sunk | while | flops 2 | bytes 12905 | solution.py:63
  239.2 3.4 multiply_reduce_fusion.2
  244.6 3.4 fusion.48
  248.0 3.6 fusion.49
  259.5 39.0 %while.20 = (s32[]{:T(128)}, f32[9,9216]{1,0:T(8,128)S(1)}, s32[32,2]{0,1:T(2,128)S(1)}, f32[32,9,128]{2,1,0:T(8,128)S(1)}, s32[]{:T(128)}) while((s32[]{:T(128)}, f32[9,9216]{1,0:T(8,128)S(1)}, s32[32,2]{0,1:T(2,128)S(1)}, f32[32,9,128]{2,1,0:T(8,128)S(1)}, s32[]{:T(128)}) %tuple.60), condition=%wide.while_cond.1, body=%wide.while_body.1.sunk | while | flops 2 | bytes 16489 | solution.py:66
  298.5 62.0 %while.21 = (s32[]{:T(128)}, f32[9,3072]{1,0:T(8,128)}, s32[32,2]{0,1:T(2,128)S(1)}, f32[32,9,128]{2,1,0:T(8,128)S(1)}, s32[]{:T(128)}) while((s32[]{:T(128)}, f32[9,3072]{1,0:T(8,128)}, s32[32,2]{0,1:T(2,128)S(1)}, f32[32,9,128]{2,1,0:T(8,128)S(1)}, s32[]{:T(128)}) %tuple.63), condition=%wide.while_cond, body=%wide.while_body.sunk | while | flops 2 | bytes 12905 | solution.py:63
  360.5 3.4 multiply_reduce_fusion.2
  365.9 3.4 fusion.48
  369.3 3.6 fusion.49
  380.8 39.0 %while.20 = (s32[]{:T(128)}, f32[9,9216]{1,0:T(8,128)S(1)}, s32[32,2]{0,1:T(2,128)S(1)}, f32[32,9,128]{2,1,0:T(8,128)S(1)}, s32[]{:T(128)}) while((s32[]{:T(128)}, f32[9,9216]{1,0:T(8,128)S(1)}, s32[32,2]{0,1:T(2,128)S(1)}, f32[32,9,128]{2,1,0:T(8,128)S(1)}, s32[]{:T(128)}) %tuple.60), condition=%wide.while_cond.1, body=%wide.while_body.1.sunk | while | flops 2 | bytes 16489 | solution.py:66
  419.9 62.0 %while.21 = (s32[]{:T(128)}, f32[9,3072]{1,0:T(8,128)}, s32[32,2]{0,1:T(2,128)S(1)}, f32[32,9,128]{2,1,0:T(8,128)S(1)}, s32[]{:T(128)}) while((s32[]{:T(128)}, f32[9,3072]{1,0:T(8,128)}, s32[32,2]{0,1:T(2,128)S(1)}, f32[32,9,128]{2,1,0:T(8,128)S(1)}, s32[]{:T(128)}) %tuple.63), condition=%wide.while_cond, body=%wide.while_body.sunk | while | flops 2 | bytes 12905 | solution.py:63
  481.9 3.4 multiply_reduce_fusion.2
  487.2 3.4 fusion.48
  490.7 3.6 fusion.49
  502.2 39.0 %while.20 = (s32[]{:T(128)}, f32[9,9216]{1,0:T(8,128)S(1)}, s32[32,2]{0,1:T(2,128)S(1)}, f32[32,9,128]{2,1,0:T(8,128)S(1)}, s32[]{:T(128)}) while((s32[]{:T(128)}, f32[9,9216]{1,0:T(8,128)S(1)}, s32[32,2]{0,1:T(2,128)S(1)}, f32[32,9,128]{2,1,0:T(8,128)S(1)}, s32[]{:T(128)}) %tuple.60), condition=%wide.while_cond.1, body=%wide.while_body.1.sunk | while | flops 2 | bytes 16489 | solution.py:66
  541.2 62.0 %while.21 = (s32[]{:T(128)}, f32[9,3072]{1,0:T(8,128)}, s32[32,2]{0,1:T(2,128)S(1)}, f32[32,9,128]{2,1,0:T(8,128)S(1)}, s32[]{:T(128)}) while((s32[]{:T(128)}, f32[9,3072]{1,0:T(8,128)}, s32[32,2]{0,1:T(2,128)S(1)}, f32[32,9,128]{2,1,0:T(8,128)S(1)}, s32[]{:T(128)}) %tuple.63), condition=%wide.while_cond, body=%wide.while_body.sunk | while | flops 2 | bytes 12905 | solution.py:63
  603.2 3.4 multiply_reduce_fusion.2
  608.5 3.4 fusion.48
  612.0 3.6 fusion.49
  623.5 39.0 %while.20 = (s32[]{:T(128)}, f32[9,9216]{1,0:T(8,128)S(1)}, s32[32,2]{0,1:T(2,128)S(1)}, f32[32,9,128]{2,1,0:T(8,128)S(1)}, s32[]{:T(128)}) while((s32[]{:T(128)}, f32[9,9216]{1,0:T(8,128)S(1)}, s32[32,2]{0,1:T(2,128)S(1)}, f32[32,9,128]{2,1,0:T(8,128)S(1)}, s32[]{:T(128)}) %tuple.60), condition=%wide.while_cond.1, body=%wide.while_body.1.sunk | while | flops 2 | bytes 16489 | solution.py:66
  662.5 62.0 %while.21 = (s32[]{:T(128)}, f32[9,3072]{1,0:T(8,128)}, s32[32,2]{0,1:T(2,128)S(1)}, f32[32,9,128]{2,1,0:T(8,128)S(1)}, s32[]{:T(128)}) while((s32[]{:T(128)}, f32[9,3072]{1,0:T(8,128)}, s32[32,2]{0,1:T(2,128)S(1)}, f32[32,9,128]{2,1,0:T(8,128)S(1)}, s32[]{:T(128)}) %tuple.63), condition=%wide.while_cond, body=%wide.while_body.sunk | while | flops 2 | bytes 12905 | solution.py:63
  724.5 3.4 multiply_reduce_fusion.2
  729.8 3.4 fusion.48
  733.3 3.6 fusion.49
  744.8 39.0 %while.20 = (s32[]{:T(128)}, f32[9,9216]{1,0:T(8,128)S(1)}, s32[32,2]{0,1:T(2,128)S(1)}, f32[32,9,128]{2,1,0:T(8,128)S(1)}, s32[]{:T(128)}) while((s32[]{:T(128)}, f32[9,9216]{1,0:T(8,128)S(1)}, s32[32,2]{0,1:T(2,128)S(1)}, f32[32,9,128]{2,1,0:T(8,128)S(1)}, s32[]{:T(128)}) %tuple.60), condition=%wide.while_cond.1, body=%wide.while_body.1.sunk | while | flops 2 | bytes 16489 | solution.py:66
  783.8 62.0 %while.21 = (s32[]{:T(128)}, f32[9,3072]{1,0:T(8,128)}, s32[32,2]{0,1:T(2,128)S(1)}, f32[32,9,128]{2,1,0:T(8,128)S(1)}, s32[]{:T(128)}) while((s32[]{:T(128)}, f32[9,3072]{1,0:T(8,128)}, s32[32,2]{0,1:T(2,128)S(1)}, f32[32,9,128]{2,1,0:T(8,128)S(1)}, s32[]{:T(128)}) %tuple.63), condition=%wide.while_cond, body=%wide.while_body.sunk | while | flops 2 | bytes 12905 | solution.py:63
  845.8 3.4 multiply_reduce_fusion.2
  851.2 3.4 fusion.48
  854.6 3.6 fusion.49
  866.1 39.0 %while.20 = (s32[]{:T(128)}, f32[9,9216]{1,0:T(8,128)S(1)}, s32[32,2]{0,1:T(2,128)S(1)}, f32[32,9,128]{2,1,0:T(8,128)S(1)}, s32[]{:T(128)}) while((s32[]{:T(128)}, f32[9,9216]{1,0:T(8,128)S(1)}, s32[32,2]{0,1:T(2,128)S(1)}, f32[32,9,128]{2,1,0:T(8,128)S(1)}, s32[]{:T(128)}) %tuple.60), condition=%wide.while_cond.1, body=%wide.while_body.1.sunk | while | flops 2 | bytes 16489 | solution.py:66
  905.1 62.0 %while.21 = (s32[]{:T(128)}, f32[9,3072]{1,0:T(8,128)}, s32[32,2]{0,1:T(2,128)S(1)}, f32[32,9,128]{2,1,0:T(8,128)S(1)}, s32[]{:T(128)}) while((s32[]{:T(128)}, f32[9,3072]{1,0:T(8,128)}, s32[32,2]{0,1:T(2,128)S(1)}, f32[32,9,128]{2,1,0:T(8,128)S(1)}, s32[]{:T(128)}) %tuple.63), condition=%wide.while_cond, body=%wide.while_body.sunk | while | flops 2 | bytes 12905 | solution.py:63
  967.1 3.4 multiply_reduce_fusion.2
  972.4 3.4 fusion.48
  975.9 3.6 fusion.49
  983.8 19.9 %scatter_custom_fusion.1 = f32[3,12288]{0,1:T(8,128)} fusion(s32[3072]{0:T(1024)S(1)} %bitcast.73, f32[3072,3]{1,0:T(8,128)S(1)} %copy.19, f32[]{:T(128)} %constant.76.clone.1), kind=kCustom, calls=%fused_computation.34 | custom fusion | flops 9216 | bytes 147460 | tf_op jit(solution)/shard_map/scatter-add | solution.py:98
  1003.7 20.6 %scatter_fusion.1 = f32[3,12288]{0,1:T(8,128)} fusion(f32[3,12288]{0,1:T(8,128)} %scatter_custom_fusion.1, s32[3072]{0:T(1024)S(1)} %bitcast.72, f32[3072,3]{1,0:T(8,128)S(1)} %copy.19), kind=kCustom, calls=%fused_computation.5 | custom fusion | flops 9216 | bytes 122880 | tf_op jit(solution)/shard_map/scatter-add | solution.py:99
  1024.4 4.4 copy.21
  1028.8 251.0 %all_to_all.5 = f32[3,4,3072]{2,0,1:T(4,128)S(1)} all-to-all(f32[3,4,3072]{2,0,1:T(4,128)S(1)} %copy.21), channel_id=1, replica_groups=mesh['col'=4,'gz'=8] {'col'}, dimensions={1} | all-to-all | bytes 294912 | tf_op jit(solution)/shard_map/all_to_all | solution.py:100
  (1703 shorter events, 887.8 us)
Async XLA Ops:
  0.0 8.1 collective-permute-start.1
  4.5 7.1 collective-permute-start
where the time goes:
time: 1300 us; the launch traced here: 1280 us
  local copies, waits for them, and re-layouts  856 us (66%)
  blocking collectives  251 us (19%)
  other arithmetic  89.3 us (7%)
  matrix products  71.7 us (6%)
    gather x1536, local copies, waits for them, and re-layouts  807 us
    all_to_all x1, blocking collectives, on_device(): lax.all_to_all(buffer.reshape(3, columns, NODE_DEV), 'col', split_axis=1,...  251 us
    dot_general x8, matrix products, pair_tile(): jnp.dot(first_block[6:9].T, second_block[6:9], precision=lax.Precision.HI...  29.1 us
    dot_general x8, matrix products, pair_tile(): jnp.dot(first_block[3:6].T, second_block[3:6], precision=lax.Precision.HI...  27.5 us
    reduce_sum x8, other arithmetic, pair_tile(): radius_sq = jnp.sum(offset * offset, axis=0) + CORE_SQ  27.3 us
  transfers between devices with their start and end apart: 2, of which 2 were waited for; matrix products, arithmetic and copies ran while one was open for 0% of the time, Pallas kernels for 0%

commit v1 on v0

v1 whole, which is shorter than its diff:
```python
import functools

import jax
import jax.numpy as jnp
from jax import lax
from jax.experimental import pallas as pl
from jax.experimental.pallas import tpu as pltpu
from jax.sharding import PartitionSpec as P

BLK = 128
NODE_DEV = 3072
MU = 0.02
CORE_SQ = 0.5

ROWS = 64
MOM = 16
GROUP = 32
TAIL = 16
BF = jnp.bfloat16
F32 = jnp.float32

_TN = (((0,), (0,)), ((), ()))
_NT = (((1,), (1,)), ((), ()))


def split3(v):
    a = v.astype(BF).astype(F32)
    r = v - a
    b = r.astype(BF).astype(F32)
    return a, b, r - b


def gather_components(seg_ref, comp, blocks):
    for b in range(blocks):
        lanes = slice(b * BLK, (b + 1) * BLK)
        comp[pl.ds(b, 8, stride=blocks), :] = seg_ref[0:8, lanes]
        comp[8 * blocks + b : 8 * blocks + b + 1, :] = seg_ref[8:9, lanes]


def features(comp, blocks):
    part = [comp[c * blocks : (c + 1) * blocks, :] for c in range(9)]
    x, burgers, line = part[0:3], part[3:6], part[6:9]
    xs = [split3(v) for v in x]
    norm = x[0] * x[0] + x[1] * x[1] + x[2] * x[2]
    prods = [split3(p * q)[0:1] + (p * q,) for p in burgers for q in line]
    prods = [(hi, full - hi) for hi, full in prods]
    return xs, norm, prods


def source_rows(xs, norm, prods):
    one = jnp.ones_like(norm)
    rows = {}
    norms = split3(norm + CORE_SQ)
    for k in range(3):
        x1, x2, x3 = xs[k]
        rows[k], rows[3 + k], rows[6 + k] = x1, x2, x3
        rows[9 + k], rows[12 + k] = one, norms[k]
        rows[15 + k], rows[18 + k], rows[21 + k] = x1, x2, x1
    for m, (hi, lo) in enumerate(prods):
        rows[32 + m], rows[41 + m], rows[50 + m] = hi, lo, hi
    return rows


def target_rows(xs, norm, prods):
    one = jnp.ones_like(norm)
    rows = {}
    norms = split3(norm)
    for k in range(3):
        x1, x2, x3 = (-2.0 * v for v in xs[k])
        rows[k], rows[3 + k], rows[6 + k] = x1, x1, x1
        rows[9 + k], rows[12 + k] = norms[k], one
        rows[15 + k], rows[18 + k], rows[21 + k] = x2, x2, x3
    for m, (hi, lo) in enumerate(prods):
        rows[32 + m], rows[41 + m], rows[50 + m] = hi, hi, lo
    return rows


def put_rows(rows, feat, blocks):
    for r in range(ROWS):
        feat[r * blocks : (r + 1) * blocks, :] = rows.get(r, jnp.zeros((blocks, BLK), F32))


def block_rows(feat, b, blocks):
    return feat[pl.ds(b, ROWS, stride=blocks), :].astype(BF)


def source_table(comp, feat, table, base, blocks):
    put_rows(source_rows(*features(comp, blocks)), feat, blocks)
    for b in range(blocks):
        table[base + b] = block_rows(feat, b, blocks)


def empty_block(table, at):
    row = lax.broadcasted_iota(jnp.int32, (ROWS, BLK), 0)
    table[at] = jnp.where(row == 12, 1.0, 0.0).astype(BF)


def pair_group(count, start, entry, target, source, forces):
    codes = [entry(start + u) for u in range(count)]
    both = [
        lax.dot_general(source[c & 127], target[c >> 7], _TN, preferred_element_type=F32)
        for c in codes
    ]
    weights = []
    for value in both:
        inverse = lax.rsqrt(value[:, :BLK])
        coupling = value[:, BLK:] * inverse * (inverse * inverse)
        hi = coupling.astype(BF)
        lo = (coupling - hi.astype(F32)).astype(BF)
        weights.append(jnp.concatenate([hi, lo], axis=0))
    for c, weight in zip(codes, weights):
        moment = source[c & 127, 0:MOM, :]
        moment = jnp.concatenate([moment, moment], axis=1)
        forces[c >> 7] += jnp.dot(moment, weight, preferred_element_type=F32)


def all_pairs(total, entry, target, source, forces):
    whole = (total + (GROUP - TAIL - 1)) // GROUP

    def step(q, carry):
        pair_group(GROUP, q * GROUP, entry, target, source, forces)
        return carry

    lax.fori_loop(0, whole, step, 0)

    @pl.when(whole * GROUP < total)
    def _():
        pair_group(TAIL, whole * GROUP, entry, target, source, forces)


def own_kernel(
    blocks, first_ref, second_ref, count_ref, seg_ref,
    target_ref, comp_ref, forces_ref, halo_list, halo_total,
    feat, source, own_list,
):
    slots = first_ref.shape[0]
    total = count_ref[0]
    empty = blocks

    def sort(p, carry):
        n_own, n_halo = carry
        first, second = first_ref[p], second_ref[p]
        own = jnp.logical_and(second >= blocks, second < 2 * blocks).astype(jnp.int32)
        listed = (p < total).astype(jnp.int32)
        shifted = second - jnp.where(second >= blocks, blocks, 0)
        code = first * 128 + shifted
        own_list[n_own] = code
        halo_list[n_halo] = code
        return n_own + own * listed, n_halo + (1 - own) * listed

    n_own, n_halo = lax.fori_loop(0, slots, sort, (0, 0), unroll=8 if slots % 8 == 0 else 1)
    for u in range(GROUP):
        own_list[n_own + u] = empty
        halo_list[n_halo + u] = 2 * blocks
    halo_total[0] = n_halo

    gather_components(seg_ref, comp_ref, blocks)
    parts = features(comp_ref, blocks)
    put_rows(source_rows(*parts), feat, blocks)
    for b in range(blocks):
        source[b] = block_rows(feat, b, blocks)
    empty_block(source, empty)
    xs, norm, prods = parts
    part = [comp_ref[c * blocks : (c + 1) * blocks, :] for c in range(3, 9)]
    scaled = [MU * p * q for p in part[0:3] for q in part[3:6]]
    scaled = [(split3(v)[0], v) for v in scaled]
    scaled = [(hi, full - hi) for hi, full in scaled]
    put_rows(target_rows(xs, norm, scaled), feat, blocks)
    blank = jnp.zeros((ROWS // 2, BLK), BF)
    for b in range(blocks):
        rows = block_rows(feat, b, blocks)
        target_ref[b, 0:32, 0:BLK] = rows[0:32]
        target_ref[b, 0:32, BLK:] = blank
        target_ref[b, 32:64, 0:BLK] = blank
        target_ref[b, 32:64, BLK:] = rows[32:64]

    forces_ref[...] = jnp.zeros_like(forces_ref)
    all_pairs(n_own, lambda p: own_list[p], target_ref, source, forces_ref)


def halo_kernel(
    blocks, codes_to, targets, halo_list, halo_total, below_ref, above_ref, target_ref, comp_ref, own_forces,
    owner_ref, slot_ref, *rest,
):
    outs, (comp, feat, source, forces, scaled, left, right, total) = rest[:targets], rest[targets:]
    for base, seg_ref in ((0, below_ref), (blocks, above_ref)):
        gather_components(seg_ref, comp, blocks)
        source_table(comp, feat, source, base, blocks)
    empty_block(source, 2 * blocks)
    forces[...] = own_forces[...]
    all_pairs(halo_total[0], lambda p: halo_list[p], target_ref, source, forces)

    flat = forces.reshape(blocks * MOM, BLK)
    row = [flat[pl.ds(m, blocks, stride=MOM), :] for m in range(10)]
    for k in range(3):
        pulled = row[k] + row[3 + k] + row[6 + k]
        half = 0.5 * (comp_ref[k * blocks : (k + 1) * blocks, :] * row[9] - pulled)
        hi = half.astype(BF).astype(F32)
        scaled[k * blocks : (k + 1) * blocks, :] = hi
        scaled[(3 + k) * blocks : (4 + k) * blocks, :] = half - hi

    highs = NODE_DEV // BLK
    span = targets * highs
    codes = owner_ref[...]
    place = jnp.zeros_like(codes)
    for code, to in enumerate(codes_to):
        if to:
            place = jnp.where(codes == code, to, place)
    slot = slot_ref[...]
    high = place * highs + (slot >> 7)
    low = slot & 127
    high_at = lax.broadcasted_iota(jnp.int32, (span, BLK), 0)
    low_at = lax.broadcasted_iota(jnp.int32, (BLK, BLK), 0)
    for b in range(blocks):
        lanes = slice(b * BLK, (b + 1) * BLK)
        values = [scaled[m * blocks + b : m * blocks + b + 1, :] for m in range(6)]
        for end in range(2):
            at = slice((2 * b + end) * BLK, (2 * b + end + 1) * BLK)
            hit = high_at == high[end : end + 1, lanes]
            right[:, at] = jnp.where(low_at == low[end : end + 1, lanes], 1.0, 0.0).astype(BF)
            for m in range(6):
                left[m * span : (m + 1) * span, at] = jnp.where(hit, values[m], 0.0).astype(BF)
    summed = lax.dot_general(left[...], right[...], _NT, preferred_element_type=F32)
    total[...] = summed[: 3 * span] + summed[3 * span :]
    for t, out in enumerate(outs):
        for h in range(highs):
            out[:, h * BLK : (h + 1) * BLK] = total[pl.ds(t * highs + h, 3, stride=span), :]


def on_device(segments, node_owner, node_slot, pair_first, pair_second, pair_count):
    width = segments.shape[1]
    blocks = width // BLK
    slots = pair_first.shape[0]
    peers = lax.axis_size("gz")
    up = [(i, (i + 1) % peers) for i in range(peers)]
    down = [(j, i) for i, j in up]
    below = lax.ppermute(segments, "gz", up)
    above = lax.ppermute(segments, "gz", down)

    smem = pl.BlockSpec(memory_space=pltpu.SMEM)
    vmem = pl.BlockSpec(memory_space=pltpu.VMEM)
    params = pltpu.CompilerParams(vmem_limit_bytes=40 << 20)
    table, comp, forces, halo_list, halo_total = pl.pallas_call(
        functools.partial(own_kernel, blocks),
        out_shape=(
            jax.ShapeDtypeStruct((blocks, ROWS, 2 * BLK), BF),
            jax.ShapeDtypeStruct((9 * blocks, BLK), F32),
            jax.ShapeDtypeStruct((blocks, MOM, BLK), F32),
            jax.ShapeDtypeStruct((slots + GROUP,), jnp.int32),
            jax.ShapeDtypeStruct((1,), jnp.int32),
        ),
        in_specs=[smem, smem, smem, vmem],
        out_specs=(vmem, vmem, vmem, smem, smem),
        scratch_shapes=[
            pltpu.VMEM((ROWS * blocks, BLK), F32),
            pltpu.VMEM((blocks + 1, ROWS, BLK), BF),
            pltpu.SMEM((slots + GROUP,), jnp.int32),
        ],
        compiler_params=params,
        cost_estimate=pl.CostEstimate(flops=10_000_000_000, bytes_accessed=1_000_000, transcendentals=0),
    )(pair_first, pair_second, pair_count, segments)

    columns = lax.axis_size("col")
    stride = columns // 4
    moves = [m % columns for m in (0, 1, -1, stride, -stride)]
    shifts = list(dict.fromkeys(moves))
    targets = len(shifts)
    span = targets * (NODE_DEV // BLK)
    partials = pl.pallas_call(
        functools.partial(halo_kernel, blocks, [shifts.index(m) for m in moves], targets),
        out_shape=tuple(jax.ShapeDtypeStruct((3, NODE_DEV), F32) for _ in shifts),
        in_specs=[smem, smem] + [vmem] * 7,
        out_specs=(vmem,) * targets,
        scratch_shapes=[
            pltpu.VMEM((9 * blocks, BLK), F32),
            pltpu.VMEM((ROWS * blocks, BLK), F32),
            pltpu.VMEM((2 * blocks + 1, ROWS, BLK), BF),
            pltpu.VMEM((blocks, MOM, BLK), F32),
            pltpu.VMEM((6 * blocks, BLK), F32),
            pltpu.VMEM((6 * span, 2 * width), BF),
            pltpu.VMEM((BLK, 2 * width), BF),
            pltpu.VMEM((3 * span, BLK), F32),
        ],
        compiler_params=params,
    )(halo_list, halo_total, below, above, table, comp, forces, node_owner, node_slot)
    node_total = partials[0]
    for shift, partial in zip(shifts[1:], partials[1:]):
        node_total = node_total + lax.ppermute(partial, "col", [(i, (i + shift) % columns) for i in range(columns)])
    return node_total


def solution(mesh):
    in_specs = (
        P(None, ("col", "gz")),
        P(None, ("col", "gz")),
        P(None, ("col", "gz")),
        P(("col", "gz")),
        P(("col", "gz")),
        P(("col", "gz")),
    )
    out_specs = P(None, ("col", "gz"))
    return jax.shard_map(
        on_device, mesh=mesh, in_specs=in_specs, out_specs=out_specs, check_vma=False
    )
```

time: 1300 us -> 32.6 us (0.03); the launches traced: 1280 us -> 32.6 us
  local copies, waits for them, and re-layouts: 856 us -> 2.29 us
  blocking collectives: 251 us -> 0 us
  other arithmetic: 89.3 us -> 0.64 us
  matrix products: 71.7 us -> 0 us
  Pallas kernels: 0 us -> 14.1 us
    gather x1560 -> x0, local copies, waits for them, and re-layouts: 835 us -> none
    all_to_all x1 -> x0, blocking collectives: 251 us -> none  [on_device(): lax.all_to_all(buffer.reshape(3, columns, NODE_DEV), 'col', split_axis=1,...]
    dot_general x24 -> x0, matrix products: 71.7 us -> none  [the longest x8 29.1 us: pair_tile(): jnp.dot(first_block[6:9].T, second_block[6:9], precision=lax.Precision.HI...]
    scatter-add x10 -> x0, other arithmetic: 53.8 us -> none  [the longest x1 20.6 us: on_device(): buffer.at[:, target(node_owner[1]) * NODE_DEV + node_slot[1]].add(halved)]
    reduce_sum x9 -> x0, other arithmetic: 28 us -> none  [the longest x8 27.3 us: pair_tile(): radius_sq = jnp.sum(offset * offset, axis=0) + CORE_SQ]
    reduce_sum x8 -> x0, local copies, waits for them, and re-layouts: 15.3 us -> none  [pair_tile(): radius_sq = jnp.sum(offset * offset, axis=0) + CORE_SQ]
    pallas_call x0 -> x2, Pallas kernels: none -> 14.1 us  [the longest x1 8.08 us: on_device(): pl.pallas_call(functools.partial(halo_kernel, blocks, [shifts.index(m) fo...]
  transfers between devices with their start and end apart: 2 -> 4, of which waited for: 2 -> 2; matrix products, arithmetic and copies ran while one was open for 0% -> 0% of each run, Pallas kernels for 0% -> 19%
where the time goes in v1:
time: 32.6 us
  Pallas kernels  14.1 us (43%)
  starting transfers between devices  10.7 us (33%)
  waiting for transfers between devices  4.09 us (13%)
  local copies, waits for them, and re-layouts  2.29 us (7%)
  between operations  0.71 us (2%)
  other arithmetic  0.64 us (2%)
    pallas_call x1, Pallas kernels, on_device(): pl.pallas_call(functools.partial(halo_kernel, blocks, [shifts.index(m) fo...  8.08 us
    ppermute x2, starting transfers between devices, on_device(): lax.ppermute(partial, 'col', [(i, (i + shift) % columns) for i in range(c...  6.23 us
    pallas_call x1, Pallas kernels, on_device(): pl.pallas_call(functools.partial(own_kernel, blocks), out_shape=(jax.Shap...  6.06 us
    ppermute x1, starting transfers between devices, on_device(): above = lax.ppermute(segments, 'gz', down)  4.49 us
    ppermute x2, waiting for transfers between devices, on_device(): lax.ppermute(partial, 'col', [(i, (i + shift) % columns) for i in range(c...  4.09 us
    unnamed x10, local copies, waits for them, and re-layouts  2.29 us
  transfers between devices with their start and end apart: 4, of which 2 were waited for; matrix products, arithmetic and copies ran while one was open for 0% of the time, Pallas kernels for 19%

profile of v1, /device:TPU:0, one launch (start us, length us, event | category | flops | bytes accessed | tf_op | source)
XLA Modules:
  0.0 32.6 jit_solution(3345578668995467448)
XLA Ops:
  0.0 4.5 %collective-permute-start.1 = (f32[9,3072]{1,0:T(8,128)}, f32[9,3072]{1,0:T(8,128)S(1)}, u32[]{:S(2)}, u32[]{:S(2)}) collective-permute-start(f32[9,3072]{1,0:T(8,128)} %seg_ref.1), channel_id=1, source_target_pairs={{1,0},{2,1},{3,2},{4,3},{5,4},{6,5},{7,6},{0,7},{9,8},{10,9},{11,1... | collective-permute-start | bytes 331784 | tf_op jit(solution)/shard_map/ppermute | solution.py:238
  4.5 0.0 collective-permute-start
  5.1 0.0 copy-start.2
  5.2 0.9 %copy-done.2 = f32[9,3072]{1,0:T(8,128)S(1)} copy-done((f32[9,3072]{1,0:T(8,128)S(1)}, f32[9,3072]{1,0:T(8,128)}, u32[]{:S(2)}) %copy-start.2) | copy-done | bytes 110616
  6.1 0.0 copy-start.3
  6.1 0.7 %copy-done.3 = s32[320]{0:T(512)S(1)} copy-done((s32[320]{0:T(512)S(1)}, s32[320]{0:T(512)}, u32[]{:S(2)}) %copy-start.3) | copy-done | bytes 1304
  6.8 0.0 copy-start.4
  6.8 0.7 %copy-done.4 = s32[320]{0:T(512)S(1)} copy-done((s32[320]{0:T(512)S(1)}, s32[320]{0:T(512)}, u32[]{:S(2)}) %copy-start.4) | copy-done | bytes 1304
  7.4 0.0 copy-start
  7.4 0.0 copy-start.1
  7.4 6.1 %shard_map.64 = (bf16[24,64,256]{2,1,0:T(8,128)(2,1)S(1)}, f32[216,128]{1,0:T(8,128)S(1)}, f32[24,16,128]{2,1,0:T(8,128)S(1)}, s32[352]{0:T(512)S(1)}, s32[1]{0:T(128)}) custom-call(s32[320]{0:T(512)S(1)} %copy-done.3, s32[320]{0:T(512)S(1)} %copy-done.4, s32[1]{0:T(128)S(6)} %copy.7.count_ref, f32[9,3072]{1,0:T(8,128)S(1)} %copy-done.2), custom_call_target="tpu_custom_call" | custom-call | flops 10000000000 | bytes 1000000 | tf_op jit(solution)/shard_map/pallas_call | solution.py:243
  13.5 0.0 collective-permute-done.1.above_ref
  13.5 0.0 collective-permute-done.below_ref
  13.5 0.0 copy-done
  13.5 0.0 copy-done.1
  13.6 8.1 %shard_map.65 = (f32[3,3072]{1,0:T(4,128)S(1)}, f32[3,3072]{1,0:T(4,128)S(1)}, f32[3,3072]{1,0:T(4,128)S(1)}) custom-call(s32[352]{0:T(512)S(1)} %get-tuple-element.13.halo_list, s32[1]{0:T(128)} %get-tuple-element.14.halo_total, f32[9,3072]{1,0:T(8,128)S(1)} %collective-permute-done.below_ref, f32[9,3072]{1,0:T(8,128)S(1)} %collective-permute-done.1.above_ref, ...), custom_call_target="tpu_custom_call" | custom-call | tf_op jit(solution)/shard_map/pallas_call | solution.py:269
  21.6 6.2 %collective-permute-start.2 = (f32[3,3072]{1,0:T(4,128)S(1)}, f32[3,3072]{1,0:T(4,128)S(1)}, u32[]{:S(2)}, u32[]{:S(2)}) collective-permute-start(f32[3,3072]{1,0:T(4,128)S(1)} %get-tuple-element.19), channel_id=1, source_target_pairs={{0,8},{8,16},{16,24},{24,0},{1,9},{9,17},{17,25},{25,1},{2,10},{10... | collective-permute-start | bytes 110600 | tf_op jit(solution)/shard_map/ppermute | solution.py:288
  27.9 0.0 collective-permute-start.3
  27.9 1.7 %collective-permute-done.2 = f32[3,3072]{1,0:T(4,128)S(1)} collective-permute-done((f32[3,3072]{1,0:T(4,128)S(1)}, f32[3,3072]{1,0:T(4,128)S(1)}, u32[]{:S(2)}, u32[]{:S(2)}) %collective-permute-start.2) | collective-permute-done | bytes 36896 | tf_op jit(solution)/shard_map/ppermute | solution.py:288
  29.6 2.3 %collective-permute-done.3 = f32[3,3072]{1,0:T(4,128)S(1)} collective-permute-done((f32[3,3072]{1,0:T(4,128)S(1)}, f32[3,3072]{1,0:T(4,128)S(1)}, u32[]{:S(2)}, u32[]{:S(2)}) %collective-permute-start.3) | collective-permute-done | bytes 36896 | tf_op jit(solution)/shard_map/ppermute | solution.py:288
  32.0 0.6 %add_add_fusion = f32[3,3072]{1,0:T(4,128)} fusion(f32[3,3072]{1,0:T(4,128)S(1)} %collective-permute-done.3, f32[3,3072]{1,0:T(4,128)S(1)} %get-tuple-element.18, f32[3,3072]{1,0:T(4,128)S(1)} %collective-permute-done.2), kind=kLoop, calls=%fused_computation | loop fusion | flops 18432 | bytes 147456 | tf_op jit(solution)/shard_map/add | solution.py:288
Async XLA Ops:
  0.0 13.5 %collective-permute-start.1 = (f32[9,3072]{1,0:T(8,128)}, f32[9,3072]{1,0:T(8,128)S(1)}, u32[]{:S(2)}, u32[]{:S(2)}) collective-permute-start(f32[9,3072]{1,0:T(8,128)} %seg_ref.1), channel_id=1, source_target_pairs={{1,0},{2,1},{3,2},{4,3},{5,4},{6,5},{7,6},{0,7},{9,8},{10,9},{11,1... | collective-permute-start | bytes 331784 | tf_op jit(solution)/shard_map/ppermute | solution.py:238
  4.5 9.0 %collective-permute-start = (f32[9,3072]{1,0:T(8,128)}, f32[9,3072]{1,0:T(8,128)S(1)}, u32[]{:S(2)}, u32[]{:S(2)}) collective-permute-start(f32[9,3072]{1,0:T(8,128)} %seg_ref.1), channel_id=1, source_target_pairs={{0,1},{1,2},{2,3},{3,4},{4,5},{5,6},{6,7},{7,0},{8,9},{9,10},{10,1... | collective-permute-start | bytes 331784 | tf_op jit(solution)/shard_map/ppermute | solution.py:237
  5.1 0.9 %copy-start.2 = (f32[9,3072]{1,0:T(8,128)S(1)}, f32[9,3072]{1,0:T(8,128)}, u32[]{:S(2)}) copy-start(f32[9,3072]{1,0:T(8,128)} %seg_ref.1) | copy-start | bytes 331780
  6.1 0.7 %copy-start.3 = (s32[320]{0:T(512)S(1)}, s32[320]{0:T(512)}, u32[]{:S(2)}) copy-start(s32[320]{0:T(512)} %first_ref.1) | copy-start | bytes 3844
  6.8 0.7 %copy-start.4 = (s32[320]{0:T(512)S(1)}, s32[320]{0:T(512)}, u32[]{:S(2)}) copy-start(s32[320]{0:T(512)} %second_ref.1) | copy-start | bytes 3844
  7.4 6.1 %copy-start = (s32[2,3072]{1,0:T(2,128)S(1)}, s32[2,3072]{1,0:T(2,128)}, u32[]{:S(2)}) copy-start(s32[2,3072]{1,0:T(2,128)} %owner_ref.1) | copy-start | bytes 73732
  7.4 6.1 %copy-start.1 = (s32[2,3072]{1,0:T(2,128)S(1)}, s32[2,3072]{1,0:T(2,128)}, u32[]{:S(2)}) copy-start(s32[2,3072]{1,0:T(2,128)} %slot_ref.1) | copy-start | bytes 73732
  21.6 8.0 %collective-permute-start.2 = (f32[3,3072]{1,0:T(4,128)S(1)}, f32[3,3072]{1,0:T(4,128)S(1)}, u32[]{:S(2)}, u32[]{:S(2)}) collective-permute-start(f32[3,3072]{1,0:T(4,128)S(1)} %get-tuple-element.19), channel_id=1, source_target_pairs={{0,8},{8,16},{16,24},{24,0},{1,9},{9,17},{17,25},{25,1},{2,10},{10... | collective-permute-start | bytes 110600 | tf_op jit(solution)/shard_map/ppermute | solution.py:288
  27.9 4.1 %collective-permute-start.3 = (f32[3,3072]{1,0:T(4,128)S(1)}, f32[3,3072]{1,0:T(4,128)S(1)}, u32[]{:S(2)}, u32[]{:S(2)}) collective-permute-start(f32[3,3072]{1,0:T(4,128)S(1)} %get-tuple-element.20), channel_id=1, source_target_pairs={{0,24},{8,0},{16,8},{24,16},{1,25},{9,1},{17,9},{25,17},{2,26},{10... | collective-permute-start | bytes 110600 | tf_op jit(solution)/shard_map/ppermute | solution.py:288

commit v2 on v1

--- a/solution.py
+++ b/solution.py
@@ -128,31 +128,40 @@
         pair_group(TAIL, whole * GROUP, entry, target, source, forces)
 
 
+def sort_pairs(blocks, packed, lists):
+    slots, places = packed.shape[1], lists.shape[1]
+    listed = packed >= 0
+    first, second = packed >> 7, packed & 127
+    inside = jnp.logical_and(second >= blocks, second < 2 * blocks)
+    own = jnp.where(jnp.logical_and(listed, inside), 1.0, 0.0)
+    halo = jnp.where(listed, 1.0, 0.0) - own
+    line = lax.broadcasted_iota(jnp.int32, (16, slots), 0)
+    member = jnp.where(line == 0, own, jnp.where(line == 1, halo, 0.0)).astype(BF)
+    before = lax.broadcasted_iota(jnp.int32, (slots, slots), 0) < lax.broadcasted_iota(jnp.int32, (slots, slots), 1)
+    rank = jnp.dot(member, jnp.where(before, 1.0, 0.0).astype(BF), preferred_element_type=F32)
+    source = second - jnp.where(second >= blocks, blocks, 0)
+    value = jnp.where(line == 0, first, jnp.where(line == 1, source, 0)).astype(F32).astype(BF)
+    place = lax.broadcasted_iota(jnp.int32, (places, slots), 0).astype(F32)
+    for r, (mine, empty) in enumerate(((own, blocks), (halo, 2 * blocks))):
+        at = jnp.where(mine > 0.0, rank[r : r + 1], -1.0)
+        hit = jnp.where(place == at, 1.0, 0.0).astype(BF)
+        found = lax.dot_general(value, hit, _NT, preferred_element_type=F32)
+        code = (found[0:1] * 128.0 + found[1:2]).astype(jnp.int32)
+        total = jnp.sum(mine, axis=1, keepdims=True).astype(jnp.int32)
+        lane = lax.broadcasted_iota(jnp.int32, (1, places), 1)
+        lists[r : r + 1, :] = jnp.where(lane < total, code, empty)
+        lists[2 + r : 3 + r, :] = jnp.broadcast_to(total, (1, places))
+
+
 def own_kernel(
-    blocks, first_ref, second_ref, count_ref, seg_ref,
-    target_ref, comp_ref, forces_ref, halo_list, halo_total,
-    feat, source, own_list,
+    blocks, packed_ref, seg_ref,
+    target_ref, comp_ref, forces_ref, lists_ref,
+    feat, source, lists, done,
 ):
-    slots = first_ref.shape[0]
-    total = count_ref[0]
     empty = blocks
-
-    def sort(p, carry):
-        n_own, n_halo = carry
-        first, second = first_ref[p], second_ref[p]
-        own = jnp.logical_and(second >= blocks, second < 2 * blocks).astype(jnp.int32)
-        listed = (p < total).astype(jnp.int32)
-        shifted = second - jnp.where(second >= blocks, blocks, 0)
-        code = first * 128 + shifted
-        own_list[n_own] = code
-        halo_list[n_halo] = code
-        return n_own + own * listed, n_halo + (1 - own) * listed
-
-    n_own, n_halo = lax.fori_loop(0, slots, sort, (0, 0), unroll=8 if slots % 8 == 0 else 1)
-    for u in range(GROUP):
-        own_list[n_own + u] = empty
-        halo_list[n_halo + u] = 2 * blocks
-    halo_total[0] = n_halo
+    sort_pairs(blocks, packed_ref[...].reshape(1, packed_ref.shape[0]), lists)
+    copy = pltpu.make_async_copy(lists, lists_ref, done.at[1])
+    copy.start()
 
     gather_components(seg_ref, comp_ref, blocks)
     parts = features(comp_ref, blocks)
@@ -175,11 +184,12 @@
         target_ref[b, 32:64, BLK:] = rows[32:64]
 
     forces_ref[...] = jnp.zeros_like(forces_ref)
-    all_pairs(n_own, lambda p: own_list[p], target_ref, source, forces_ref)
+    copy.wait()
+    all_pairs(lists_ref[2, 0], lambda p: lists_ref[0, p], target_ref, source, forces_ref)
 
 
 def halo_kernel(
-    blocks, codes_to, targets, halo_list, halo_total, below_ref, above_ref, target_ref, comp_ref, own_forces,
+    blocks, codes_to, targets, lists_ref, below_ref, above_ref, target_ref, comp_ref, own_forces,
     owner_ref, slot_ref, *rest,
 ):
     outs, (comp, feat, source, forces, scaled, left, right, total) = rest[:targets], rest[targets:]
@@ -188,7 +198,7 @@
         source_table(comp, feat, source, base, blocks)
     empty_block(source, 2 * blocks)
     forces[...] = own_forces[...]
-    all_pairs(halo_total[0], lambda p: halo_list[p], target_ref, source, forces)
+    all_pairs(lists_ref[3, 0], lambda p: lists_ref[1, p], target_ref, source, forces)
 
     flat = forces.reshape(blocks * MOM, BLK)
     row = [flat[pl.ds(m, blocks, stride=MOM), :] for m in range(10)]
@@ -231,34 +241,38 @@
     width = segments.shape[1]
     blocks = width // BLK
     slots = pair_first.shape[0]
+    places = -(-(slots + GROUP) // BLK) * BLK
     peers = lax.axis_size("gz")
     up = [(i, (i + 1) % peers) for i in range(peers)]
     down = [(j, i) for i, j in up]
     below = lax.ppermute(segments, "gz", up)
     above = lax.ppermute(segments, "gz", down)
 
+    listed = jnp.arange(slots, dtype=jnp.int32) < pair_count[0]
+    packed = jnp.where(listed, pair_first * 128 + pair_second, -1)
+
     smem = pl.BlockSpec(memory_space=pltpu.SMEM)
     vmem = pl.BlockSpec(memory_space=pltpu.VMEM)
     params = pltpu.CompilerParams(vmem_limit_bytes=40 << 20)
-    table, comp, forces, halo_list, halo_total = pl.pallas_call(
+    table, comp, forces, lists = pl.pallas_call(
         functools.partial(own_kernel, blocks),
         out_shape=(
             jax.ShapeDtypeStruct((blocks, ROWS, 2 * BLK), BF),
             jax.ShapeDtypeStruct((9 * blocks, BLK), F32),
             jax.ShapeDtypeStruct((blocks, MOM, BLK), F32),
-            jax.ShapeDtypeStruct((slots + GROUP,), jnp.int32),
-            jax.ShapeDtypeStruct((1,), jnp.int32),
+            jax.ShapeDtypeStruct((8, places), jnp.int32),
         ),
-        in_specs=[smem, smem, smem, vmem],
-        out_specs=(vmem, vmem, vmem, smem, smem),
+        in_specs=[vmem, vmem],
+        out_specs=(vmem, vmem, vmem, smem),
         scratch_shapes=[
             pltpu.VMEM((ROWS * blocks, BLK), F32),
             pltpu.VMEM((blocks + 1, ROWS, BLK), BF),
-            pltpu.SMEM((slots + GROUP,), jnp.int32),
+            pltpu.VMEM((8, places), jnp.int32),
+            pltpu.SemaphoreType.DMA((2,)),
         ],
         compiler_params=params,
         cost_estimate=pl.CostEstimate(flops=10_000_000_000, bytes_accessed=1_000_000, transcendentals=0),
-    )(pair_first, pair_second, pair_count, segments)
+    )(packed, segments)
 
     columns = lax.axis_size("col")
     stride = columns // 4
@@ -269,7 +283,7 @@
     partials = pl.pallas_call(
         functools.partial(halo_kernel, blocks, [shifts.index(m) for m in moves], targets),
         out_shape=tuple(jax.ShapeDtypeStruct((3, NODE_DEV), F32) for _ in shifts),
-        in_specs=[smem, smem] + [vmem] * 7,
+        in_specs=[smem] + [vmem] * 7,
         out_specs=(vmem,) * targets,
         scratch_shapes=[
             pltpu.VMEM((9 * blocks, BLK), F32),
@@ -282,7 +296,7 @@
             pltpu.VMEM((3 * span, BLK), F32),
         ],
         compiler_params=params,
-    )(halo_list, halo_total, below, above, table, comp, forces, node_owner, node_slot)
+    )(lists, below, above, table, comp, forces, node_owner, node_slot)
     node_total = partials[0]
     for shift, partial in zip(shifts[1:], partials[1:]):
         node_total = node_total + lax.ppermute(partial, "col", [(i, (i + shift) % columns) for i in range(columns)])

time: 32.6 us -> 28.8 us (0.88)
  Pallas kernels: 14.1 us -> 10.3 us
  waiting for transfers between devices: 4.09 us -> 5.61 us
  local copies, waits for them, and re-layouts: 2.29 us -> 0.94 us
  starting transfers between devices: 10.7 us -> 10 us
  other arithmetic: 0.64 us -> 1.33 us
    pallas_call x1, Pallas kernels: 6.06 us -> 3.69 us  [on_device(): pl.pallas_call(functools.partial(own_kernel, blocks), out_shape=(jax.Shap...]
    pallas_call x1, Pallas kernels: 8.08 us -> 6.57 us  [on_device(): pl.pallas_call(functools.partial(halo_kernel, blocks, [shifts.index(m) fo...]
    unnamed x10 -> x8, local copies, waits for them, and re-layouts: 2.29 us -> 0.94 us
    ppermute x1, waiting for transfers between devices: 0.01 us -> 1.11 us  [on_device(): below = lax.ppermute(segments, 'gz', up)]
    select_n x0 -> x1, other arithmetic: none -> 0.69 us  [on_device(): packed = jnp.where(listed, pair_first * 128 + pair_second, -1)]
    ppermute x2, starting transfers between devices: 6.23 us -> 5.55 us  [on_device(): lax.ppermute(partial, 'col', [(i, (i + shift) % columns) for i in range(c...]
    ppermute x2, waiting for transfers between devices: 4.09 us -> 4.49 us  [on_device(): lax.ppermute(partial, 'col', [(i, (i + shift) % columns) for i in range(c...]
  transfers between devices with their start and end apart: 4 -> 4, of which waited for: 2 -> 3; matrix products, arithmetic and copies ran while one was open for 0% -> 2% of each run, Pallas kernels for 19% -> 13%
where the time goes in v2:
time: 28.8 us; the launch traced here: 28.9 us
  Pallas kernels  10.3 us (36%)
  starting transfers between devices  10 us (35%)
  waiting for transfers between devices  5.61 us (19%)
  other arithmetic  1.33 us (5%)
  local copies, waits for them, and re-layouts  0.94 us (3%)
  between operations  0.69 us (2%)
    pallas_call x1, Pallas kernels, on_device(): pl.pallas_call(functools.partial(halo_kernel, blocks, [shifts.index(m) fo...  6.57 us
    ppermute x2, starting transfers between devices, on_device(): lax.ppermute(partial, 'col', [(i, (i + shift) % columns) for i in range(c...  5.55 us
    ppermute x2, waiting for transfers between devices, on_device(): lax.ppermute(partial, 'col', [(i, (i + shift) % columns) for i in range(c...  4.49 us
    ppermute x1, starting transfers between devices, on_device(): above = lax.ppermute(segments, 'gz', down)  4.49 us
    pallas_call x1, Pallas kernels, on_device(): pl.pallas_call(functools.partial(own_kernel, blocks), out_shape=(jax.Shap...  3.69 us
    ppermute x1, waiting for transfers between devices, on_device(): below = lax.ppermute(segments, 'gz', up)  1.11 us
    unnamed x8, local copies, waits for them, and re-layouts  0.94 us
    select_n x1, other arithmetic, on_device(): packed = jnp.where(listed, pair_first * 128 + pair_second, -1)  0.69 us
  transfers between devices with their start and end apart: 4, of which 3 were waited for; matrix products, arithmetic and copies ran while one was open for 2% of the time, Pallas kernels for 13%

profile of v2, /device:TPU:0, one launch (start us, length us, event | category | flops | bytes accessed | tf_op | source)
XLA Modules:
  0.0 28.9 jit_solution(15090696136978830810)
XLA Ops:
  0.0 0.0 copy-start.3
  0.0 4.5 %collective-permute-start.1 = (f32[9,3072]{1,0:T(8,128)}, f32[9,3072]{1,0:T(8,128)S(1)}, u32[]{:S(2)}, u32[]{:S(2)}) collective-permute-start(f32[9,3072]{1,0:T(8,128)} %seg_ref.1), channel_id=1, source_target_pairs={{1,0},{2,1},{3,2},{4,3},{5,4},{6,5},{7,6},{0,7},{9,8},{10,9},{11,1... | collective-permute-start | bytes 331784 | tf_op jit(solution)/shard_map/ppermute | solution.py:249
  4.5 0.0 collective-permute-start
  5.1 0.0 copy-done.3
  5.2 0.7 %add_select_fusion.packed_ref = s32[320]{0:T(512)S(1)} fusion(s32[320]{0:T(512)S(1)} %copy-done.3, s32[320]{0:T(512)} %param.9, s32[]{:T(128)} %bitcast.1), kind=kLoop, calls=%fused_computation.1 | loop fusion | flops 1280 | bytes 3844 | tf_op jit(solution)/shard_map/jit(_where)/select_n | solution.py:252
  5.8 0.0 copy-start.2
  5.8 0.9 %copy-done.2 = f32[9,3072]{1,0:T(8,128)S(1)} copy-done((f32[9,3072]{1,0:T(8,128)S(1)}, f32[9,3072]{1,0:T(8,128)}, u32[]{:S(2)}) %copy-start.2) | copy-done | bytes 110616
  6.8 0.0 copy-start
  6.8 0.0 copy-start.1
  6.8 3.7 %shard_map.64 = (bf16[24,64,256]{2,1,0:T(8,128)(2,1)S(1)}, f32[216,128]{1,0:T(8,128)S(1)}, f32[24,16,128]{2,1,0:T(8,128)S(1)}, s32[8,384]{1,0:T(8,128)S(1)}) custom-call(s32[320]{0:T(512)S(1)} %add_select_fusion.packed_ref, f32[9,3072]{1,0:T(8,128)S(1)} %copy-done.2), custom_call_target="tpu_custom_call" | custom-call | flops 10000000000 | bytes 1000000 | tf_op jit(solution)/shard_map/pallas_call | solution.py:257
  10.5 0.0 collective-permute-done.1.above_ref
  10.5 1.1 %collective-permute-done.below_ref = f32[9,3072]{1,0:T(8,128)S(1)} collective-permute-done((f32[9,3072]{1,0:T(8,128)}, f32[9,3072]{1,0:T(8,128)S(1)}, u32[]{:S(2)}, u32[]{:S(2)}) %collective-permute-start) | collective-permute-done | bytes 110624 | tf_op jit(solution)/shard_map/ppermute | solution.py:248
  11.6 0.0 copy-done
  11.6 0.0 copy-done.1
  11.6 6.6 %shard_map.65 = (f32[3,3072]{1,0:T(4,128)S(1)}, f32[3,3072]{1,0:T(4,128)S(1)}, f32[3,3072]{1,0:T(4,128)S(1)}) custom-call(s32[8,384]{1,0:T(8,128)S(1)} %get-tuple-element.12.lists_ref, f32[9,3072]{1,0:T(8,128)S(1)} %collective-permute-done.below_ref, f32[9,3072]{1,0:T(8,128)S(1)} %collective-permute-done.1.above_ref, ...), custom_call_target="tpu_custom_call" | custom-call | tf_op jit(solution)/shard_map/pallas_call | solution.py:283
  18.2 3.6 %collective-permute-start.2 = (f32[3,3072]{1,0:T(4,128)S(1)}, f32[3,3072]{1,0:T(4,128)S(1)}, u32[]{:S(2)}, u32[]{:S(2)}) collective-permute-start(f32[3,3072]{1,0:T(4,128)S(1)} %get-tuple-element.17), channel_id=1, source_target_pairs={{0,8},{8,16},{16,24},{24,0},{1,9},{9,17},{17,25},{25,1},{2,10},{10... | collective-permute-start | bytes 110600 | tf_op jit(solution)/shard_map/ppermute | solution.py:302
  21.8 2.0 %collective-permute-start.3 = (f32[3,3072]{1,0:T(4,128)S(1)}, f32[3,3072]{1,0:T(4,128)S(1)}, u32[]{:S(2)}, u32[]{:S(2)}) collective-permute-start(f32[3,3072]{1,0:T(4,128)S(1)} %get-tuple-element.18), channel_id=1, source_target_pairs={{0,24},{8,0},{16,8},{24,16},{1,25},{9,1},{17,9},{25,17},{2,26},{10... | collective-permute-start | bytes 110600 | tf_op jit(solution)/shard_map/ppermute | solution.py:302
  23.7 2.5 %collective-permute-done.2 = f32[3,3072]{1,0:T(4,128)S(1)} collective-permute-done((f32[3,3072]{1,0:T(4,128)S(1)}, f32[3,3072]{1,0:T(4,128)S(1)}, u32[]{:S(2)}, u32[]{:S(2)}) %collective-permute-start.2) | collective-permute-done | bytes 36896 | tf_op jit(solution)/shard_map/ppermute | solution.py:302
  26.3 2.0 %collective-permute-done.3 = f32[3,3072]{1,0:T(4,128)S(1)} collective-permute-done((f32[3,3072]{1,0:T(4,128)S(1)}, f32[3,3072]{1,0:T(4,128)S(1)}, u32[]{:S(2)}, u32[]{:S(2)}) %collective-permute-start.3) | collective-permute-done | bytes 36896 | tf_op jit(solution)/shard_map/ppermute | solution.py:302
  28.2 0.6 %add_add_fusion = f32[3,3072]{1,0:T(4,128)} fusion(f32[3,3072]{1,0:T(4,128)S(1)} %collective-permute-done.3, f32[3,3072]{1,0:T(4,128)S(1)} %get-tuple-element.16, f32[3,3072]{1,0:T(4,128)S(1)} %collective-permute-done.2), kind=kLoop, calls=%fused_computation | loop fusion | flops 18432 | bytes 147456 | tf_op jit(solution)/shard_map/add | solution.py:302
Async XLA Ops:
  0.0 5.1 %copy-start.3 = (s32[320]{0:T(512)S(1)}, s32[320]{0:T(512)}, u32[]{:S(2)}) copy-start(s32[320]{0:T(512)} %param.10) | copy-start | bytes 3844
  0.0 10.5 %collective-permute-start.1 = (f32[9,3072]{1,0:T(8,128)}, f32[9,3072]{1,0:T(8,128)S(1)}, u32[]{:S(2)}, u32[]{:S(2)}) collective-permute-start(f32[9,3072]{1,0:T(8,128)} %seg_ref.1), channel_id=1, source_target_pairs={{1,0},{2,1},{3,2},{4,3},{5,4},{6,5},{7,6},{0,7},{9,8},{10,9},{11,1... | collective-permute-start | bytes 331784 | tf_op jit(solution)/shard_map/ppermute | solution.py:249
  4.5 7.1 %collective-permute-start = (f32[9,3072]{1,0:T(8,128)}, f32[9,3072]{1,0:T(8,128)S(1)}, u32[]{:S(2)}, u32[]{:S(2)}) collective-permute-start(f32[9,3072]{1,0:T(8,128)} %seg_ref.1), channel_id=1, source_target_pairs={{0,1},{1,2},{2,3},{3,4},{4,5},{5,6},{6,7},{7,0},{8,9},{9,10},{10,1... | collective-permute-start | bytes 331784 | tf_op jit(solution)/shard_map/ppermute | solution.py:248
  5.8 0.9 %copy-start.2 = (f32[9,3072]{1,0:T(8,128)S(1)}, f32[9,3072]{1,0:T(8,128)}, u32[]{:S(2)}) copy-start(f32[9,3072]{1,0:T(8,128)} %seg_ref.1) | copy-start | bytes 331780
  6.8 4.8 %copy-start = (s32[2,3072]{1,0:T(2,128)S(1)}, s32[2,3072]{1,0:T(2,128)}, u32[]{:S(2)}) copy-start(s32[2,3072]{1,0:T(2,128)} %owner_ref.1) | copy-start | bytes 73732
  6.8 4.8 %copy-start.1 = (s32[2,3072]{1,0:T(2,128)S(1)}, s32[2,3072]{1,0:T(2,128)}, u32[]{:S(2)}) copy-start(s32[2,3072]{1,0:T(2,128)} %slot_ref.1) | copy-start | bytes 73732
  18.2 8.1 %collective-permute-start.2 = (f32[3,3072]{1,0:T(4,128)S(1)}, f32[3,3072]{1,0:T(4,128)S(1)}, u32[]{:S(2)}, u32[]{:S(2)}) collective-permute-start(f32[3,3072]{1,0:T(4,128)S(1)} %get-tuple-element.17), channel_id=1, source_target_pairs={{0,8},{8,16},{16,24},{24,0},{1,9},{9,17},{17,25},{25,1},{2,10},{10... | collective-permute-start | bytes 110600 | tf_op jit(solution)/shard_map/ppermute | solution.py:302
  21.8 6.5 %collective-permute-start.3 = (f32[3,3072]{1,0:T(4,128)S(1)}, f32[3,3072]{1,0:T(4,128)S(1)}, u32[]{:S(2)}, u32[]{:S(2)}) collective-permute-start(f32[3,3072]{1,0:T(4,128)S(1)} %get-tuple-element.18), channel_id=1, source_target_pairs={{0,24},{8,0},{16,8},{24,16},{1,25},{9,1},{17,9},{25,17},{2,26},{10... | collective-permute-start | bytes 110600 | tf_op jit(solution)/shard_map/ppermute | solution.py:302
